TPU v7x, 128 devices: a whole 4x4x4 slice. The times are simulated.
128 devices in a mesh: rep: 32 (over z, y, x_lo), row: 2 (over core), col: 2 (over x_hi).
Axes of the slice: x: 4 (x_hi: 2, x_lo: 2; x = x_hi * 2 + x_lo), y: 4, z: 4, core: 2. Of those that a mesh axis runs over, the one named last changes fastest.
Arguments:
- fronts: bfloat16 [32, 6144, 6144], P('rep', 'row', 'col'), may hold values from -8 to 72, as said below
- lower_mask: int32 [32, 2, 24], P('rep'), may hold values 0 or 1
- upper_mask: int32 [32, 2, 24], P('rep'), may hold values 0 or 1
Outputs:
- ancestors: float32 [2, 32, 96, 6144], P('row', 'rep', None, 'col')
Inputs may be any that keep to these rules, and one draw needn't show every extreme that they name: `fronts`: entries are of order one except on the diagonals of the pivot blocks of g0 and g1, which carry 4 * sqrt(256) more.
All inputs are finite; a program needn't handle non-finite values. No bound on the sum of `lower_mask` or of `upper_mask` on one device may be relied on, other than what follows from the above.
Results may differ from a plain program's by a relative error of at most 0.04.
Values may be sent and summed in bfloat16 or wider, within the bound.
A program may use at most 384 MiB of HBM per device.

v0:
```python
import jax
import jax.numpy as jnp
from jax import lax
from jax.experimental import pallas as pl
from jax.experimental.pallas import tpu as pltpu
from jax.sharding import PartitionSpec as P

W = 256
NB = 24
ROWS = 3072
SHARE = 96
UNIT = 128
BLOCKS = 11
SLOTS = 3
SLABS = 4
STEPS = BLOCKS + 5
MIB = 2**20
MESH = pl.DeviceIdType.MESH
F32 = jnp.float32
BF16 = jnp.bfloat16


def dot(left, right):
    return jnp.dot(left, right, preferred_element_type=F32)


def split(value):
    high = value.astype(BF16)
    return high, (value - high.astype(F32)).astype(BF16)


def place():
    rep, row, col = (lax.axis_index(name) for name in ("rep", "row", "col"))
    return rep // 8, (rep // 2) % 4, rep % 2, row, col


def device(z, y, x, row, col):
    return {"rep": z * 8 + y * 2 + x, "row": row, "col": col}


def gather_kernel(front, corners, strips, send_sem, recv_sem, copy_sem):
    z, y, x, row, col = place()
    beside = device(z, y, x, 1 - row, col)
    across = device(z, y, x, row, 1 - col)
    barrier = pltpu.get_barrier_semaphore()
    for peer in (beside, across):
        pl.semaphore_signal(barrier, inc=1, device_id=peer, device_id_type=MESH)
    pl.semaphore_wait(barrier, 2)
    corner = front.at[pl.ds(row * W, W), pl.ds(col * W, W)]
    strip = front.at[pl.ds(row * W, W), :]

    def remote(src, dst, index, peer):
        return pltpu.make_async_remote_copy(
            src_ref=src, dst_ref=dst, send_sem=send_sem.at[index], recv_sem=recv_sem.at[index],
            device_id=peer, device_id_type=MESH)

    mine = row * 2 + col
    first = remote(corner, corners.at[mine], 0, across)
    first.start()
    second = remote(corner, corners.at[mine], 1, beside)
    second.start()
    third = remote(strip, strips.at[row], 2, beside)
    third.start()
    own_corner = pltpu.make_async_copy(corner, corners.at[mine], copy_sem.at[0])
    own_corner.start()
    own_strip = pltpu.make_async_copy(strip, strips.at[row], copy_sem.at[1])
    own_strip.start()
    first.wait_recv()
    theirs = row * 2 + 1 - col
    fourth = remote(corners.at[theirs], corners.at[theirs], 3, beside)
    fourth.start()
    first.wait_send()
    second.wait()
    third.wait()
    fourth.wait()
    own_corner.wait()
    own_strip.wait()


def invert(pivot, pivot_high, pivot_low, high, low, work):
    rows = lax.broadcasted_iota(jnp.int32, (W, W), 0)
    cols = lax.broadcasted_iota(jnp.int32, (W, W), 1)
    eye = rows == cols
    ones = jnp.where(eye, 1.0, 0.0)
    diag = jnp.where(eye, pivot, 0.0)
    down = jnp.sum(diag, axis=1, keepdims=True)
    along = jnp.sum(diag, axis=0, keepdims=True)
    rest = jnp.where(eye, 0.0, -pivot / along)
    rest_low = rest.astype(BF16)
    guess = (ones + rest) / down
    two = dot(rest_low, rest_low).astype(BF16)
    four = dot(two, two).astype(BF16)
    guess = guess + dot(guess.astype(BF16), two)
    guess = guess + dot(guess.astype(BF16), four)
    guess_high, guess_low = split(guess)
    product = dot(pivot_high, guess_high) + dot(pivot_high, guess_low)
    if pivot_low is not None:
        product = product + dot(pivot_low, guess_high)
    residual = ones - product
    guess = guess + dot(guess_high, residual.astype(BF16))
    size = jnp.max(jnp.sum(jnp.abs(residual), axis=1))
    good = size < 0.03
    work[...] = guess

    @pl.when(jnp.logical_not(good))
    def _():
        work[...] = pivot

        def step(k, carry):
            here = work[...]
            across = work[pl.ds(k, 1), :]
            column = jnp.sum(jnp.where(cols == k, here, 0.0), axis=1, keepdims=True)
            lane = lax.broadcasted_iota(jnp.int32, (1, W), 1) == k
            value = jnp.sum(jnp.where(lane, across, 0.0), axis=1, keepdims=True)
            scaled = jnp.where(lane, 1.0, across) / value
            here = jnp.where(cols == k, 0.0, here) - column * scaled
            work[...] = jnp.where(rows == k, scaled, here)
            return carry

        lax.fori_loop(0, W, step, 0)

    result_high, result_low = split(work[...])
    high[...] = result_high
    low[...] = result_low


def factor_kernel(lower_mask, upper_mask, corners, strips, zero_high, zero_low, one_high, one_low,
                  corner_up, upper, work):
    col = lax.axis_index("col")
    invert(corners[0].astype(F32), corners[0], None, zero_high, zero_low, work)
    keep_low = lower_mask[0, 0, NB // 2 + 1].astype(F32)
    keep_up = upper_mask[0, 0, NB // 2 + 1].astype(F32)
    below = dot(corners[2], zero_high[...]) + dot(corners[2], zero_low[...])
    below = (below * keep_low).astype(BF16)
    right = (corners[1].astype(F32) * keep_up).astype(BF16)
    corner_up[...] = right
    pivot = corners[3].astype(F32) - dot(below, right)
    pivot_high, pivot_low = split(pivot)
    invert(pivot, pivot_high, pivot_low, one_high, one_low, work)
    for block in range(NB // 2):
        span = pl.ds(block * W, W)
        mask_zero = upper_mask[0, 0, col * (NB // 2) + block].astype(F32)
        mask_one = upper_mask[0, 1, col * (NB // 2) + block].astype(F32)
        top = (strips[0, :, span].astype(F32) * mask_zero).astype(BF16)
        upper[0:W, span] = top
        under = strips[1, :, span].astype(F32) - dot(below, top)
        upper[W:2 * W, span] = (under * mask_one).astype(BF16)


def reduce_kernel(lower_mask, front, upper, zero_high, zero_low, one_high, one_low, corner_up, out,
                  panel, lower, slab, snd_one, rcv_one, snd_two, rcv_two, snd_wide, rcv_wide,
                  snd_last, rcv_last, held_one, held_two,
                  panel_sem, slab_sem, snd_one_sem, rcv_one_sem, snd_two_sem, rcv_two_sem,
                  snd_last_sem, rcv_last_sem):
    z, y, x, row, col = place()

    def at_z(k):
        return device((z + k + 4) % 4, y, x, row, col)

    def at_y(k):
        return device(z, (y + k + 4) % 4, x, row, col)

    pair = device(z, y, 1 - x, row, col)
    across = device(z, y, x, row, 1 - col)
    barrier = pltpu.get_barrier_semaphore()
    for peer in (at_z(1), at_z(-1), at_y(1), at_y(-1), pair, across):
        pl.semaphore_signal(barrier, inc=1, device_id=peer, device_id_type=MESH)
    pl.semaphore_wait(barrier, 6)

    order = [(z + k) % 4 for k in (2, 3, 1, 0)]

    def panel_copies(k, quarter):
        source = front.at[quarter, :, :, pl.ds(pl.multiple_of(col * W, W), W)]
        own = pltpu.make_async_copy(source, panel.at[col, quarter], panel_sem.at[0, k])
        remote = pltpu.make_async_remote_copy(
            src_ref=source, dst_ref=panel.at[col, quarter], send_sem=panel_sem.at[1, k],
            recv_sem=panel_sem.at[2, k], device_id=across, device_id_type=MESH)
        return own, remote

    for k in range(4):
        own, remote = panel_copies(k, order[k])
        own.start()
        remote.start()

    def offset(block):
        start = W * (block + 1) - W * col * (1 - jnp.minimum(block, 1))
        return pl.multiple_of(start, W)

    def slab_copy(block):
        return pltpu.make_async_copy(
            front.at[:, :, :, pl.ds(offset(block), W)], slab.at[block % SLABS],
            slab_sem.at[block % SLABS])

    slab_copy(0).start()

    for k in range(4):
        quarter = order[k]
        own, remote = panel_copies(k, quarter)
        own.wait()
        remote.wait()
        left_all = panel[0, quarter].reshape(768, W)
        next_all = panel[1, quarter].reshape(768, W)
        low_zero, low_one = [], []
        for part in range(3):
            span = slice(part * W, part * W + W)
            block = row * (NB // 2) + quarter * 3 + part
            mask_zero = lower_mask[0, 0, block].astype(F32)
            mask_one = lower_mask[0, 1, block].astype(F32)
            first = dot(left_all[span], zero_high[...]) + dot(left_all[span], zero_low[...])
            first = (first * mask_zero).astype(BF16)
            column = next_all[span].astype(F32) - dot(first, corner_up[...])
            column_high, column_low = split(column)
            second = (dot(column_high, one_high[...]) + dot(column_high, one_low[...])
                      + dot(column_low, one_high[...]))
            low_zero.append(first)
            low_one.append((second * mask_one).astype(BF16))
        lower[quarter, :, :, 0:W] = jnp.concatenate(low_zero, axis=0).reshape(4, 192, W)
        lower[quarter, :, :, W:2 * W] = jnp.concatenate(low_one, axis=0).reshape(4, 192, W)

    first_at = (at_z, at_y)
    second_at = (at_y, at_z)
    first_pos = (z, y)
    second_pos = (y, z)

    def way(stream, block):
        turn = 1 - 2 * ((block + stream) % 2)
        return turn

    def product(stream, block, dest):
        span = pl.ds(pl.multiple_of(offset(block) + stream * UNIT, UNIT), UNIT)
        held = block % SLABS
        lanes = slice(stream * UNIT, stream * UNIT + UNIT)
        if stream == 0:
            left = lower[dest]
            here = slab[held, dest, :, :, lanes]
        else:
            left = lower[:, dest]
            here = slab[held, :, dest, :, lanes]
        value = here.reshape(768, UNIT).astype(F32) - dot(left.reshape(768, 2 * W), upper[:, span])
        return value

    def copy_one(stream, kind, block):
        turn = way(stream, block)
        peer = first_at[stream](turn if kind < 2 else -turn)
        return pltpu.make_async_remote_copy(
            src_ref=snd_one.at[stream, kind, block % SLOTS], dst_ref=rcv_one.at[stream, kind, block],
            send_sem=snd_one_sem.at[stream, kind, block % SLOTS],
            recv_sem=rcv_one_sem.at[stream, kind, block], device_id=peer, device_id_type=MESH)

    def send_one(stream, kind, block, value):
        @pl.when(block >= SLOTS)
        def _():
            copy_one(stream, kind, block - SLOTS).wait_send()
        snd_one[stream, kind, block % SLOTS] = value.astype(BF16).reshape(4, 192, UNIT)
        copy_one(stream, kind, block).start()

    def copy_two(stream, kind, block):
        turn = way(stream, block)
        peer = second_at[stream](turn if kind < 2 else -turn)
        if kind == 0:
            src, dst = snd_two.at[stream, block % SLOTS], rcv_two.at[stream, block]
        else:
            src = snd_wide.at[stream, kind - 1, block % SLOTS]
            dst = rcv_wide.at[stream, kind - 1, block]
        return pltpu.make_async_remote_copy(
            src_ref=src, dst_ref=dst, send_sem=snd_two_sem.at[stream, kind, block % SLOTS],
            recv_sem=rcv_two_sem.at[stream, kind, block], device_id=peer, device_id_type=MESH)

    def send_two(stream, kind, block, value):
        @pl.when(block >= SLOTS)
        def _():
            copy_two(stream, kind, block - SLOTS).wait_send()
        if kind == 0:
            snd_two[stream, block % SLOTS] = value.astype(BF16)
        else:
            snd_wide[stream, kind - 1, block % SLOTS] = value
        copy_two(stream, kind, block).start()

    def copy_last(stream, block):
        return pltpu.make_async_remote_copy(
            src_ref=snd_last.at[stream, block % SLOTS], dst_ref=rcv_last.at[stream, block],
            send_sem=snd_last_sem.at[stream, block % SLOTS],
            recv_sem=rcv_last_sem.at[stream, block], device_id=pair, device_id_type=MESH)

    def start_unit(stream, block):
        turn = way(stream, block)
        pos = first_pos[stream]
        send_one(stream, 0, block, product(stream, block, (pos + 2) % 4))
        send_one(stream, 2, block, product(stream, block, (pos - turn + 4) % 4))

    def pass_unit(stream, block):
        turn = way(stream, block)
        pos = first_pos[stream]
        value = product(stream, block, (pos + turn + 4) % 4)
        copy_one(stream, 0, block).wait_recv()
        value = value + rcv_one[stream, 0, block].reshape(768, UNIT).astype(F32)
        send_one(stream, 1, block, value)

    def close_unit(stream, block):
        turn = way(stream, block)
        value = product(stream, block, first_pos[stream])
        copy_one(stream, 2, block).wait_recv()
        value = value + rcv_one[stream, 2, block].reshape(768, UNIT).astype(F32)
        copy_one(stream, 1, block).wait_recv()
        value = value + rcv_one[stream, 1, block].reshape(768, UNIT).astype(F32)
        slot = block % SLABS
        held_one[stream, slot] = value.reshape(4, 192, UNIT)
        pos = second_pos[stream]
        send_two(stream, 0, block, held_one[stream, slot, (pos + 2) % 4])
        send_two(stream, 2, block, held_one[stream, slot, (pos - turn + 4) % 4])

    def pass_sum(stream, block):
        turn = way(stream, block)
        copy_two(stream, 0, block).wait_recv()
        value = held_one[stream, block % SLABS, (second_pos[stream] + turn + 4) % 4]
        send_two(stream, 1, block, value + rcv_two[stream, block].astype(F32))

    def close_sum(stream, block):
        copy_two(stream, 2, block).wait_recv()
        copy_two(stream, 1, block).wait_recv()
        value = held_one[stream, block % SLABS, second_pos[stream]]
        value = value + rcv_wide[stream, 0, block] + rcv_wide[stream, 1, block]
        held_two[stream, block % SLOTS] = value.reshape(2, SHARE, UNIT)

        @pl.when(block >= SLOTS)
        def _():
            copy_last(stream, block - SLOTS).wait_send()
        snd_last[stream, block % SLOTS] = held_two[stream, block % SLOTS, 1 - x]
        copy_last(stream, block).start()

    cells = (z * 8 + y * 2 + x) * SHARE + lax.broadcasted_iota(jnp.int32, (SHARE, UNIT), 0)
    live = (cells < row * W) | (cells >= row * W + W)

    def finish(stream, block):
        copy_last(stream, block).wait_recv()
        value = held_two[stream, block % SLOTS, x] + rcv_last[stream, block]
        span = pl.ds(pl.multiple_of(offset(block) + stream * UNIT, UNIT), UNIT)
        out[:, span] = jnp.where(live, value, 0.0)

    out[:, pl.ds(pl.multiple_of(col * W, W), W)] = jnp.zeros((SHARE, W), F32)

    def when(low, block, function):
        @pl.when((block >= 0) & (block < BLOCKS))
        def _():
            for stream in (0, 1):
                function(stream, block)

    def step(now, carry):
        @pl.when(now < BLOCKS)
        def _():
            slab_copy(now).wait()

        @pl.when(now + 1 < BLOCKS)
        def _():
            slab_copy(now + 1).start()

        when(0, now, start_unit)
        when(1, now - 1, pass_unit)
        when(2, now - 2, close_unit)
        when(3, now - 3, pass_sum)
        when(4, now - 4, close_sum)
        when(5, now - 5, finish)
        return carry

    lax.fori_loop(0, STEPS, step, 0)

    def drain(block, carry):
        for stream in (0, 1):
            for kind in range(3):
                copy_one(stream, kind, block).wait_send()
                copy_two(stream, kind, block).wait_send()
            copy_last(stream, block).wait_send()
        return carry

    lax.fori_loop(BLOCKS - SLOTS, BLOCKS, drain, 0)


def local(fronts, lower_mask, upper_mask):
    any_space = pl.BlockSpec(memory_space=pl.ANY)
    vmem = pl.BlockSpec(memory_space=pltpu.VMEM)
    smem = pl.BlockSpec(memory_space=pltpu.SMEM)
    front = fronts.reshape(ROWS, ROWS)
    corners, strips = pl.pallas_call(
        gather_kernel,
        out_shape=[jax.ShapeDtypeStruct((4, W, W), BF16), jax.ShapeDtypeStruct((2, W, ROWS), BF16)],
        in_specs=[any_space],
        out_specs=[vmem, vmem],
        scratch_shapes=[pltpu.SemaphoreType.DMA((4,)), pltpu.SemaphoreType.DMA((4,)),
                        pltpu.SemaphoreType.DMA((2,))],
        compiler_params=pltpu.CompilerParams(collective_id=0, has_side_effects=True,
                                             vmem_limit_bytes=24 * MIB),
        name="gather_corners",
    )(front)
    block = jax.ShapeDtypeStruct((W, W), BF16)
    factors = pl.pallas_call(
        factor_kernel,
        out_shape=[block] * 5 + [jax.ShapeDtypeStruct((2 * W, ROWS), BF16)],
        in_specs=[smem, smem, vmem, vmem],
        out_specs=[vmem] * 6,
        scratch_shapes=[pltpu.VMEM((W, W), F32)],
        compiler_params=pltpu.CompilerParams(vmem_limit_bytes=32 * MIB),
        name="invert_pivots",
    )(lower_mask, upper_mask, corners, strips)
    zero_high, zero_low, one_high, one_low, corner_up, upper = factors
    dma = pltpu.SemaphoreType.DMA
    out = pl.pallas_call(
        reduce_kernel,
        out_shape=jax.ShapeDtypeStruct((SHARE, ROWS), F32),
        in_specs=[smem, any_space] + [vmem] * 6,
        out_specs=vmem,
        scratch_shapes=[
            pltpu.VMEM((2, 4, 4, 192, W), BF16),
            pltpu.VMEM((4, 4, 192, 2 * W), BF16),
            pltpu.VMEM((SLABS, 4, 4, 192, W), BF16),
            pltpu.VMEM((2, 3, SLOTS, 4, 192, UNIT), BF16),
            pltpu.VMEM((2, 3, BLOCKS, 4, 192, UNIT), BF16),
            pltpu.VMEM((2, SLOTS, 192, UNIT), BF16),
            pltpu.VMEM((2, BLOCKS, 192, UNIT), BF16),
            pltpu.VMEM((2, 2, SLOTS, 192, UNIT), F32),
            pltpu.VMEM((2, 2, BLOCKS, 192, UNIT), F32),
            pltpu.VMEM((2, SLOTS, SHARE, UNIT), F32),
            pltpu.VMEM((2, BLOCKS, SHARE, UNIT), F32),
            pltpu.VMEM((2, SLABS, 4, 192, UNIT), F32),
            pltpu.VMEM((2, SLOTS, 2, SHARE, UNIT), F32),
            dma((3, 4)), dma((SLABS,)), dma((2, 3, SLOTS)), dma((2, 3, BLOCKS)),
            dma((2, 3, SLOTS)), dma((2, 3, BLOCKS)), dma((2, SLOTS)), dma((2, BLOCKS)),
        ],
        compiler_params=pltpu.CompilerParams(collective_id=1, has_side_effects=True,
                                             vmem_limit_bytes=60 * MIB),
        name="reduce_layers",
    )(lower_mask, front.reshape(4, 4, 192, ROWS), upper, zero_high, zero_low, one_high, one_low,
      corner_up)
    return out.reshape(1, 1, SHARE, ROWS)


def solution(mesh):
    in_specs = (P("rep", "row", "col"), P("rep", None, None), P("rep", None, None))
    out_specs = P("row", "rep", None, "col")
    return jax.shard_map(local, mesh=mesh, in_specs=in_specs, out_specs=out_specs, check_vma=False)
```

profile of v0, /device:TPU:0, one launch (start us, length us, event | category | flops | bytes accessed | tf_op | source)
XLA Modules:
  0.0 249.8 jit_solution(2828724644004353970)
XLA Ops:
  0.0 0.0 copy-start
  0.0 6.4 %copy-done = bf16[1,3072,3072]{2,1,0:T(8,128)(2,1)S(1)} copy-done((bf16[1,3072,3072]{2,1,0:T(8,128)(2,1)S(1)}, bf16[1,3072,3072]{2,1,0:T(8,128)(2,1)}, u32[]{:S(2)}) %copy-start) | copy-done | bytes 18874392
  6.4 0.0 copy-start.7
  6.4 0.0 copy-start.8
  6.4 8.4 %gather_corners.1 = (bf16[4,256,256]{2,1,0:T(8,128)(2,1)S(1)}, bf16[2,256,3072]{2,1,0:T(8,128)(2,1)S(1)}) custom-call(bf16[3072,3072]{1,0:T(8,128)(2,1)S(1)} %bitcast.4), custom_call_target="tpu_custom_call" | custom-call | tf_op jit(solution)/shard_map/gather_corners/pallas_call | solution.py:383
  14.7 0.0 copy-done.7
  14.7 0.0 copy-done.8
  14.8 70.0 %invert_pivots.1 = (bf16[256,256]{1,0:T(8,128)(2,1)S(1)}, bf16[256,256]{1,0:T(8,128)(2,1)S(1)}, bf16[256,256]{1,0:T(8,128)(2,1)S(1)}, bf16[256,256]{1,0:T(8,128)...) custom-call(s32[1,2,24]{2,1,0:T(2,128)S(1)} %copy-done.7, s32[1,2,24]{2,1,0:T(2,128)S(1)} %copy-done.8, ...), custom_call_target="tpu_custom_call" | custom-call | tf_op jit(solution)/shard_map/invert_pivots/pallas_call | solution.py:395
  84.8 0.0 copy-start.1
  84.8 1.6 copy-done.1
  86.4 0.0 copy-start.2
  86.4 0.7 copy-done.2
  87.0 0.0 copy-start.3
  87.0 0.7 copy-done.3
  87.7 0.0 copy-start.4
  87.7 0.7 copy-done.4
  88.4 0.0 copy-start.5
  88.4 0.7 copy-done.5
  89.0 0.0 copy-start.6
  89.0 0.6 copy-done.6
  89.7 157.8 %reduce_layers.1 = f32[96,3072]{1,0:T(8,128)} custom-call(s32[1,2,24]{2,1,0:T(2,128)} %lower_mask.3, bf16[4,4,192,3072]{3,2,1,0:T(8,128)(2,1)} %bitcast.3, bf16[512,3072]{1,0:T(8,128)(2,1)} %copy-done.1, bf16[256,256]{1,0:T(8,128)(2,1)} %copy-done.2, bf16[256,256]{1,0:T(8,128)(2,1)} %copy-done.3, bf16[256,256]{1,0:T(8,128)(2,1)} %copy-done.4, ...), custom_call_target="tpu_custom_call" | custom-call | tf_op jit(solution)/shard_map/reduce_layers/pallas_call | solution.py:406
  247.5 2.4 copy.5
Async XLA Ops:
  0.0 6.4 %copy-start = (bf16[1,3072,3072]{2,1,0:T(8,128)(2,1)S(1)}, bf16[1,3072,3072]{2,1,0:T(8,128)(2,1)}, u32[]{:S(2)}) copy-start(bf16[1,3072,3072]{2,1,0:T(8,128)(2,1)} %param.3) | copy-start | bytes 56623108
  6.4 8.4 %copy-start.7 = (s32[1,2,24]{2,1,0:T(2,128)S(1)}, s32[1,2,24]{2,1,0:T(2,128)}, u32[]{:S(2)}) copy-start(s32[1,2,24]{2,1,0:T(2,128)} %lower_mask.3) | copy-start | bytes 580
  6.4 8.4 %copy-start.8 = (s32[1,2,24]{2,1,0:T(2,128)S(1)}, s32[1,2,24]{2,1,0:T(2,128)}, u32[]{:S(2)}) copy-start(s32[1,2,24]{2,1,0:T(2,128)} %upper_mask.1) | copy-start | bytes 580
  84.8 1.6 copy-start.1
  86.4 0.7 copy-start.2
  87.0 0.7 copy-start.3
  87.7 0.7 copy-start.4
  88.4 0.7 copy-start.5
  89.0 0.6 copy-start.6
where the time goes:
time: 250 us
  Pallas kernels  236 us (94%)
  local copies, waits for them, and re-layouts  13.6 us (5%)
    pallas_call x1, Pallas kernels, local(): pl.pallas_call(reduce_kernel, out_shape=jax.ShapeDtypeStruct((SHARE, ROWS...  158 us
    pallas_call x1, Pallas kernels, local(): pl.pallas_call(factor_kernel, out_shape=[block] * 5 + [jax.ShapeDtypeStru...  70 us
    unnamed x19, local copies, waits for them, and re-layouts  13.6 us
    pallas_call x1, Pallas kernels, local(): pl.pallas_call(gather_kernel, out_shape=[jax.ShapeDtypeStruct((4, W, W),...  8.35 us

commit v1 on v0

v1 whole, which is shorter than its diff:
```python
import jax
import jax.numpy as jnp
from jax import lax
from jax.experimental import pallas as pl
from jax.experimental.pallas import tpu as pltpu
from jax.sharding import PartitionSpec as P

W = 256
NB = 24
ROWS = 3072
SHARE = 96
UNIT = 128
BLOCKS = 11
SLOTS = 3
LAGS = (2, 3, 4, 5)
MIB = 2**20
MESH = pl.DeviceIdType.MESH
F32 = jnp.float32
BF16 = jnp.bfloat16


def dot(left, right):
    return jnp.dot(left, right, preferred_element_type=F32)


def split(value):
    high = value.astype(BF16)
    return high, (value - high.astype(F32)).astype(BF16)


def place():
    rep, row, col = (lax.axis_index(name) for name in ("rep", "row", "col"))
    return rep // 8, (rep // 2) % 4, rep % 2, row, col


def device(z, y, x, row, col):
    return {"rep": z * 8 + y * 2 + x, "row": row, "col": col}


def gather_kernel(front, corners, strip_far, send_sem, recv_sem, copy_sem):
    z, y, x, row, col = place()
    beside = device(z, y, x, 1 - row, col)
    across = device(z, y, x, row, 1 - col)
    barrier = pltpu.get_barrier_semaphore()
    for peer in (beside, across):
        pl.semaphore_signal(barrier, inc=1, device_id=peer, device_id_type=MESH)
    pl.semaphore_wait(barrier, 2)
    corner = front.at[pl.ds(row * W, W), pl.ds(col * W, W)]
    strip = front.at[pl.ds(row * W, W), :]

    def remote(src, dst, index, peer):
        return pltpu.make_async_remote_copy(
            src_ref=src, dst_ref=dst, send_sem=send_sem.at[index], recv_sem=recv_sem.at[index],
            device_id=peer, device_id_type=MESH)

    mine = row * 2 + col
    first = remote(corner, corners.at[mine], 0, across)
    first.start()
    second = remote(corner, corners.at[mine], 1, beside)
    second.start()
    third = remote(strip, strip_far, 2, beside)
    third.start()
    own_corner = pltpu.make_async_copy(corner, corners.at[mine], copy_sem.at[0])
    own_corner.start()
    first.wait_recv()
    theirs = row * 2 + 1 - col
    fourth = remote(corners.at[theirs], corners.at[theirs], 3, beside)
    fourth.start()
    first.wait_send()
    second.wait()
    third.wait()
    fourth.wait()
    own_corner.wait()


def invert(pivot, pivot_high, pivot_low, high, low, work):
    rows = lax.broadcasted_iota(jnp.int32, (W, W), 0)
    cols = lax.broadcasted_iota(jnp.int32, (W, W), 1)
    eye = rows == cols
    ones = jnp.where(eye, 1.0, 0.0)
    diag = jnp.where(eye, pivot, 0.0)
    down = jnp.sum(diag, axis=1, keepdims=True)
    along = jnp.sum(diag, axis=0, keepdims=True)
    rest = jnp.where(eye, 0.0, -pivot / along)
    rest_low = rest.astype(BF16)
    guess = (ones + rest) / down
    two = dot(rest_low, rest_low).astype(BF16)
    four = dot(two, two).astype(BF16)
    guess = guess + dot(guess.astype(BF16), two)
    guess = guess + dot(guess.astype(BF16), four)
    guess_high, guess_low = split(guess)
    product = dot(pivot_high, guess_high) + dot(pivot_high, guess_low)
    if pivot_low is not None:
        product = product + dot(pivot_low, guess_high)
    residual = ones - product
    guess = guess + dot(guess_high, residual.astype(BF16))
    size = jnp.max(jnp.sum(jnp.abs(residual), axis=1))
    good = size < 0.03
    work[...] = guess

    @pl.when(jnp.logical_not(good))
    def _():
        work[...] = pivot

        def step(k, carry):
            here = work[...]
            across = work[pl.ds(k, 1), :]
            column = jnp.sum(jnp.where(cols == k, here, 0.0), axis=1, keepdims=True)
            lane = lax.broadcasted_iota(jnp.int32, (1, W), 1) == k
            value = jnp.sum(jnp.where(lane, across, 0.0), axis=1, keepdims=True)
            scaled = jnp.where(lane, 1.0, across) / value
            here = jnp.where(cols == k, 0.0, here) - column * scaled
            work[...] = jnp.where(rows == k, scaled, here)
            return carry

        lax.fori_loop(0, W, step, 0)

    result_high, result_low = split(work[...])
    high[...] = result_high
    low[...] = result_low


def factor_kernel(lower_mask, upper_mask, front, corners, strip_far, factors, upper_far, work,
                  strips, upper, in_sem, out_sem):
    row, col = lax.axis_index("row"), lax.axis_index("col")

    def strip_copy(part):
        if part == 0:
            source, slot = front.at[pl.ds(pl.multiple_of(row * W, W), W), :], row
        else:
            source, slot = strip_far, 1 - row
        return pltpu.make_async_copy(source, strips.at[slot], in_sem.at[part])

    def upper_copy(block):
        span = pl.ds(block * W, W)
        return pltpu.make_async_copy(upper.at[:, span], upper_far.at[:, span], out_sem.at[block])

    for part in range(2):
        strip_copy(part).start()
    zero_high, zero_low, one_high, one_low = (factors.at[k] for k in range(4))
    invert(corners[0].astype(F32), corners[0], None, zero_high, zero_low, work)
    keep_low = lower_mask[0, 0, NB // 2 + 1].astype(F32)
    keep_up = upper_mask[0, 0, NB // 2 + 1].astype(F32)
    below = dot(corners[2], zero_high[...]) + dot(corners[2], zero_low[...])
    below = (below * keep_low).astype(BF16)
    right = (corners[1].astype(F32) * keep_up).astype(BF16)
    factors[4] = right
    for part in range(2):
        strip_copy(part).wait()
    for block in range(NB // 2):
        span = pl.ds(block * W, W)
        mask_zero = upper_mask[0, 0, col * (NB // 2) + block].astype(F32)
        mask_one = upper_mask[0, 1, col * (NB // 2) + block].astype(F32)
        top = (strips[0, :, span].astype(F32) * mask_zero).astype(BF16)
        upper[0:W, span] = top
        under = strips[1, :, span].astype(F32) - dot(below, top)
        upper[W:2 * W, span] = (under * mask_one).astype(BF16)
        upper_copy(block).start()
    pivot = corners[3].astype(F32) - dot(below, right)
    pivot_high, pivot_low = split(pivot)
    invert(pivot, pivot_high, pivot_low, one_high, one_low, work)
    for block in range(NB // 2):
        upper_copy(block).wait()


def reduce_kernel(lower_mask, front, upper_far, factors, out,
                  upper, lower, tile, snd_first, snd_one, rcv_one, snd_two, rcv_two, snd_wide,
                  rcv_wide, snd_last, rcv_last, held_one, held_two,
                  upper_sem, panel_sem, tile_sem, snd_first_sem, snd_one_sem, rcv_one_sem,
                  snd_two_sem, rcv_two_sem, snd_last_sem, rcv_last_sem):
    z, y, x, row, col = place()

    def at_z(k):
        return device((z + k + 4) % 4, y, x, row, col)

    def at_y(k):
        return device(z, (y + k + 4) % 4, x, row, col)

    first_at = (at_z, at_y)
    second_at = (at_y, at_z)
    first_pos = (z, y)
    second_pos = (y, z)
    pair = device(z, y, 1 - x, row, col)
    across = device(z, y, x, row, 1 - col)
    upper_copy = pltpu.make_async_copy(upper_far, upper, upper_sem.at[0])
    upper_copy.start()

    def offset(block):
        start = W * (block + 1) - W * col * (1 - jnp.minimum(block, 1))
        return pl.multiple_of(start, W)

    def dest_of(stream, kind):
        return (first_pos[stream] + (2, 1, 3, 0)[kind]) % 4

    def tile_copy(stream, kind, i):
        dest, span = dest_of(stream, kind), pl.ds(offset(2 * i + stream), W)
        source = front.at[dest, :, :, span] if stream == 0 else front.at[:, dest, :, span]
        return pltpu.make_async_copy(source, tile.at[stream, kind, i % 2],
                                     tile_sem.at[stream, kind, i % 2])

    for kind in range(4):
        for stream in range(2):
            tile_copy(stream, kind, 0).start()

    barrier = pltpu.get_barrier_semaphore()
    for peer in (at_z(1), at_z(-1), at_y(1), at_y(-1), pair, across):
        pl.semaphore_signal(barrier, inc=1, device_id=peer, device_id_type=MESH)
    pl.semaphore_wait(barrier, 6)

    def piece_copies(dz, dy):
        at, by = (z + dz) % 4, (y + dy) % 4
        span = pl.ds(pl.multiple_of(col * W, W), W)
        source = front.at[at, by, :, span]
        target = lower.at[at, by, :, span]
        own = pltpu.make_async_copy(source, target, panel_sem.at[0, dz, dy])
        remote = pltpu.make_async_remote_copy(
            src_ref=source, dst_ref=target, send_sem=panel_sem.at[1, dz, dy],
            recv_sem=panel_sem.at[2, dz, dy], device_id=across, device_id_type=MESH)
        return own, remote

    def send_piece(dz, dy):
        own, remote = piece_copies(dz, dy)
        own.start()
        remote.start()

    def make_piece(dz, dy):
        own, remote = piece_copies(dz, dy)
        own.wait()
        remote.wait()
        at, by = (z + dz) % 4, (y + dy) % 4
        cell = by * 192 + lax.broadcasted_iota(jnp.int32, (192, W), 0)

        def keep(section):
            first = row * (NB // 2) + at * 3
            flags = [lower_mask[0, section, first + part].astype(F32) for part in range(3)]
            return jnp.where(cell < W, flags[0], jnp.where(cell < 2 * W, flags[1], flags[2]))

        left = lower[at, by, :, 0:W]
        column = lower[at, by, :, W:2 * W].astype(F32)
        first = dot(left, factors[0]) + dot(left, factors[1])
        first = (first * keep(0)).astype(BF16)
        column_high, column_low = split(column - dot(first, factors[4]))
        second = (dot(column_high, factors[2]) + dot(column_high, factors[3])
                  + dot(column_low, factors[2]))
        lower[at, by, :, 0:W] = first
        lower[at, by, :, W:2 * W] = (second * keep(1)).astype(BF16)

    def pieces(count, spot, function):
        def body(k, carry):
            function(*spot(k))
            return carry
        lax.fori_loop(0, count, body, 0)

    groups = (
        (4, lambda k: (2, k)),
        (3, lambda k: ((k + 3) % 4, 2)),
        (9, lambda k: ((1 + 2 * (k // 3) + 3 * (k // 6)) % 4, (k % 3 + 3) % 4)),
    )
    for count, spot in groups:
        pieces(count, spot, send_piece)

    def product(stream, kind, i):
        @pl.when(2 * (i + 1) + stream < BLOCKS)
        def _():
            tile_copy(stream, kind, i + 1).start()
        dest = dest_of(stream, kind)
        left = lower[dest] if stream == 0 else lower[:, dest]
        update = dot(left.reshape(768, 2 * W), upper[:, pl.ds(offset(2 * i + stream), W)])
        tile_copy(stream, kind, i).wait()
        return tile[stream, kind, i % 2].reshape(768, W).astype(F32) - update

    def half_of(value, half):
        return value[:, half * UNIT:half * UNIT + UNIT]

    def peer_of(places_of, half, kind):
        turn = 1 - 2 * half
        return places_of(turn if kind < 2 else -turn)

    def copy_one(stream, kind, half, i):
        if kind == 0:
            src, sem = snd_first.at[half, 2 * i + stream], snd_first_sem.at[half, 2 * i + stream]
        else:
            src = snd_one.at[stream, kind - 1, half, i % SLOTS]
            sem = snd_one_sem.at[stream, kind - 1, half, i % SLOTS]
        return pltpu.make_async_remote_copy(
            src_ref=src, dst_ref=rcv_one.at[kind, half, 2 * i + stream], send_sem=sem,
            recv_sem=rcv_one_sem.at[kind, half, 2 * i + stream],
            device_id=peer_of(first_at[stream], half, kind), device_id_type=MESH)

    def send_one(stream, kind, half, i, value):
        value = value.astype(BF16).reshape(4, 192, UNIT)
        if kind == 0:
            snd_first[half, 2 * i + stream] = value
        else:
            @pl.when(i >= SLOTS)
            def _():
                copy_one(stream, kind, half, i - SLOTS).wait_send()
            snd_one[stream, kind - 1, half, i % SLOTS] = value
        copy_one(stream, kind, half, i).start()

    def got_one(stream, kind, half, i):
        copy_one(stream, kind, half, i).wait_recv()
        return rcv_one[kind, half, 2 * i + stream].reshape(768, UNIT).astype(F32)

    def copy_two(stream, kind, half, i):
        if kind == 0:
            src, dst = snd_two.at[stream, half, i % SLOTS], rcv_two.at[half, 2 * i + stream]
        else:
            src = snd_wide.at[stream, kind - 1, half, i % SLOTS]
            dst = rcv_wide.at[kind - 1, half, 2 * i + stream]
        return pltpu.make_async_remote_copy(
            src_ref=src, dst_ref=dst, send_sem=snd_two_sem.at[stream, kind, half, i % SLOTS],
            recv_sem=rcv_two_sem.at[kind, half, 2 * i + stream],
            device_id=peer_of(second_at[stream], half, kind), device_id_type=MESH)

    def send_two(stream, kind, half, i, value):
        @pl.when(i >= SLOTS)
        def _():
            copy_two(stream, kind, half, i - SLOTS).wait_send()
        if kind == 0:
            snd_two[stream, half, i % SLOTS] = value.astype(BF16)
        else:
            snd_wide[stream, kind - 1, half, i % SLOTS] = value
        copy_two(stream, kind, half, i).start()

    def copy_last(stream, i):
        return pltpu.make_async_remote_copy(
            src_ref=snd_last.at[stream, i % SLOTS], dst_ref=rcv_last.at[2 * i + stream],
            send_sem=snd_last_sem.at[stream, i % SLOTS], recv_sem=rcv_last_sem.at[2 * i + stream],
            device_id=pair, device_id_type=MESH)

    def open_block(stream, i):
        value = product(stream, 0, i)
        for half in range(2):
            send_one(stream, 0, half, i, half_of(value, half))

    def pass_block(stream, i):
        for kind, half in ((1, 0), (2, 1)):
            value = product(stream, kind, i)
            send_one(stream, 2, 1 - half, i, half_of(value, 1 - half))
            send_one(stream, 1, half, i, half_of(value, half) + got_one(stream, 0, half, i))

    def close_block(stream, i):
        value = product(stream, 3, i)
        for half in range(2):
            part = half_of(value, half) + got_one(stream, 2, half, i) + got_one(stream, 1, half, i)
            held_one[stream, i % SLOTS, half] = part.reshape(4, 192, UNIT)
        for half in range(2):
            pos, turn = second_pos[stream], 1 - 2 * half
            send_two(stream, 0, half, i, held_one[stream, i % SLOTS, half, (pos + 2) % 4])
            send_two(stream, 2, half, i, held_one[stream, i % SLOTS, half, (pos - turn + 4) % 4])

    def pass_sum(stream, i):
        for half in range(2):
            pos, turn = second_pos[stream], 1 - 2 * half
            copy_two(stream, 0, half, i).wait_recv()
            value = held_one[stream, i % SLOTS, half, (pos + turn + 4) % 4]
            send_two(stream, 1, half, i, value + rcv_two[half, 2 * i + stream].astype(F32))

    def close_sum(stream, i):
        for half in range(2):
            copy_two(stream, 2, half, i).wait_recv()
            copy_two(stream, 1, half, i).wait_recv()
            value = held_one[stream, i % SLOTS, half, second_pos[stream]]
            value = value + rcv_wide[0, half, 2 * i + stream] + rcv_wide[1, half, 2 * i + stream]
            lanes = slice(half * UNIT, half * UNIT + UNIT)
            held_two[stream, i % SLOTS, :, :, lanes] = value.reshape(2, SHARE, UNIT)

        @pl.when(i >= SLOTS)
        def _():
            copy_last(stream, i - SLOTS).wait_send()
        snd_last[stream, i % SLOTS] = held_two[stream, i % SLOTS, 1 - x]
        copy_last(stream, i).start()

    cells = (z * 8 + y * 2 + x) * SHARE + lax.broadcasted_iota(jnp.int32, (SHARE, W), 0)
    live = (cells < row * W) | (cells >= row * W + W)

    def finish(stream, i):
        copy_last(stream, i).wait_recv()
        value = held_two[stream, i % SLOTS, x] + rcv_last[2 * i + stream]
        out[:, pl.ds(offset(2 * i + stream), W)] = jnp.where(live, value, 0.0)

    counts = ((BLOCKS + 1) // 2, BLOCKS // 2)

    def open_all(stream):
        def body(i, carry):
            open_block(stream, i)
            return carry
        lax.fori_loop(0, counts[stream], body, 0)

    pieces(*groups[0], make_piece)
    upper_copy.wait()
    open_all(0)
    pieces(*groups[1], make_piece)
    open_all(1)
    pieces(*groups[2], make_piece)
    out[:, pl.ds(pl.multiple_of(col * W, W), W)] = jnp.zeros((SHARE, W), F32)

    def when(function, stream, i):
        @pl.when((i >= 0) & (i < counts[stream]))
        def _():
            function(stream, i)

    stages = (pass_block, close_block, pass_sum, close_sum, finish)

    def step(i, carry):
        for half in range(2):
            for stage, lag in zip(stages, (0,) + LAGS):
                stream = (half - lag) % 2
                when(stage, stream, i + (half - lag - stream) // 2)
        return carry

    lax.fori_loop(0, (BLOCKS + LAGS[-1] + 1) // 2, step, 0)

    for stream in range(2):
        def drain_first(i, carry):
            for half in range(2):
                copy_one(stream, 0, half, i).wait_send()
            return carry
        lax.fori_loop(0, counts[stream], drain_first, 0)
        for i in range(counts[stream] - SLOTS, counts[stream]):
            for half in range(2):
                for kind in range(3):
                    if kind:
                        copy_one(stream, kind, half, i).wait_send()
                    copy_two(stream, kind, half, i).wait_send()
            copy_last(stream, i).wait_send()


def local(fronts, lower_mask, upper_mask):
    any_space = pl.BlockSpec(memory_space=pl.ANY)
    vmem = pl.BlockSpec(memory_space=pltpu.VMEM)
    smem = pl.BlockSpec(memory_space=pltpu.SMEM)
    front = fronts.reshape(ROWS, ROWS)
    dma = pltpu.SemaphoreType.DMA
    corners, strip = pl.pallas_call(
        gather_kernel,
        out_shape=[jax.ShapeDtypeStruct((4, W, W), BF16), jax.ShapeDtypeStruct((W, ROWS), BF16)],
        in_specs=[any_space],
        out_specs=[vmem, vmem],
        scratch_shapes=[dma((4,)), dma((4,)), dma((1,))],
        compiler_params=pltpu.CompilerParams(collective_id=0, has_side_effects=True,
                                             vmem_limit_bytes=60 * MIB),
        name="gather_corners",
    )(front)
    factors, upper = pl.pallas_call(
        factor_kernel,
        out_shape=[jax.ShapeDtypeStruct((5, W, W), BF16),
                   jax.ShapeDtypeStruct((2 * W, ROWS), BF16)],
        in_specs=[smem, smem, any_space, vmem, any_space],
        out_specs=[vmem, any_space],
        scratch_shapes=[pltpu.VMEM((W, W), F32), pltpu.VMEM((2, W, ROWS), BF16),
                        pltpu.VMEM((2 * W, ROWS), BF16), dma((2,)), dma((NB // 2,))],
        compiler_params=pltpu.CompilerParams(vmem_limit_bytes=60 * MIB),
        name="invert_pivots",
    )(lower_mask, upper_mask, front, corners, strip)
    out = pl.pallas_call(
        reduce_kernel,
        out_shape=jax.ShapeDtypeStruct((SHARE, ROWS), F32),
        in_specs=[smem, any_space, any_space, vmem],
        out_specs=vmem,
        scratch_shapes=[
            pltpu.VMEM((2 * W, ROWS), BF16),
            pltpu.VMEM((4, 4, 192, 2 * W), BF16),
            pltpu.VMEM((2, 4, 2, 4, 192, W), BF16),
            pltpu.VMEM((2, BLOCKS, 4, 192, UNIT), BF16),
            pltpu.VMEM((2, 2, 2, SLOTS, 4, 192, UNIT), BF16),
            pltpu.VMEM((3, 2, BLOCKS, 4, 192, UNIT), BF16),
            pltpu.VMEM((2, 2, SLOTS, 192, UNIT), BF16),
            pltpu.VMEM((2, BLOCKS, 192, UNIT), BF16),
            pltpu.VMEM((2, 2, 2, SLOTS, 192, UNIT), F32),
            pltpu.VMEM((2, 2, BLOCKS, 192, UNIT), F32),
            pltpu.VMEM((2, SLOTS, SHARE, W), F32),
            pltpu.VMEM((BLOCKS, SHARE, W), F32),
            pltpu.VMEM((2, SLOTS, 2, 4, 192, UNIT), F32),
            pltpu.VMEM((2, SLOTS, 2, SHARE, W), F32),
            dma((1,)), dma((3, 4, 4)), dma((2, 4, 2)), dma((2, BLOCKS)), dma((2, 2, 2, SLOTS)),
            dma((3, 2, BLOCKS)), dma((2, 3, 2, SLOTS)), dma((3, 2, BLOCKS)), dma((2, SLOTS)),
            dma((BLOCKS,)),
        ],
        compiler_params=pltpu.CompilerParams(collective_id=1, has_side_effects=True,
                                             vmem_limit_bytes=60 * MIB),
        name="reduce_layers",
    )(lower_mask, front.reshape(4, 4, 192, ROWS), upper, factors)
    return out.reshape(1, 1, SHARE, ROWS)


def solution(mesh):
    in_specs = (P("rep", "row", "col"), P("rep", None, None), P("rep", None, None))
    out_specs = P("row", "rep", None, "col")
    return jax.shard_map(local, mesh=mesh, in_specs=in_specs, out_specs=out_specs, check_vma=False)
```

time: 250 us -> 221 us (0.88)
  Pallas kernels: 236 us -> 218 us
  local copies, waits for them, and re-layouts: 13.6 us -> 2.36 us
    pallas_call x1, Pallas kernels: 158 us -> 136 us  [local(): pl.pallas_call(reduce_kernel, out_shape=jax.ShapeDtypeStruct((SHARE, ROWS...]
    unnamed x19 -> x1, local copies, waits for them, and re-layouts: 13.6 us -> 2.36 us
where the time goes in v1:
time: 221 us; the launch traced here: 220 us
  Pallas kernels  218 us (99%)
  local copies, waits for them, and re-layouts  2.36 us (1%)
    pallas_call x1, Pallas kernels, local(): pl.pallas_call(reduce_kernel, out_shape=jax.ShapeDtypeStruct((SHARE, ROWS...  136 us
    pallas_call x1, Pallas kernels, local(): pl.pallas_call(factor_kernel, out_shape=[jax.ShapeDtypeStruct((5, W, W),...  71.6 us
    pallas_call x1, Pallas kernels, local(): pl.pallas_call(gather_kernel, out_shape=[jax.ShapeDtypeStruct((4, W, W),...  9.89 us

profile of v1, /device:TPU:0, one launch (start us, length us, event | category | flops | bytes accessed | tf_op | source)
XLA Modules:
  0.0 220.0 jit_solution(11688732000392339989)
XLA Ops:
  0.0 9.9 %gather_corners.1 = (bf16[4,256,256]{2,1,0:T(8,128)(2,1)}, bf16[256,3072]{1,0:T(8,128)(2,1)}) custom-call(bf16[3072,3072]{1,0:T(8,128)(2,1)} %bitcast.3), custom_call_target="tpu_custom_call" | custom-call | tf_op jit(solution)/shard_map/gather_corners/pallas_call | solution.py:436
  9.9 71.6 %invert_pivots.1 = (bf16[5,256,256]{2,1,0:T(8,128)(2,1)}, bf16[512,3072]{1,0:T(8,128)(2,1)}) custom-call(s32[1,2,24]{2,1,0:T(2,128)} %lower_mask.3, s32[1,2,24]{2,1,0:T(2,128)} %upper_mask.1, bf16[3072,3072]{1,0:T(8,128)(2,1)} %bitcast.4, bf16[4,256,256]{2,1,0:T(8,128)(2,1)} %get-tuple-element.9.corners, bf16[256,3072]{1,0:T(8,128)(2,1)} %get-tuple-element.10.strip_far), custom_call_target="tpu_custom_call" | custom-call | tf_op jit(solution)/shard_map/invert_pivots/pallas_call | solution.py:446
  81.5 136.1 %reduce_layers.1 = f32[96,3072]{1,0:T(8,128)} custom-call(s32[1,2,24]{2,1,0:T(2,128)} %lower_mask.3, bf16[4,4,192,3072]{3,2,1,0:T(8,128)(2,1)} %bitcast.5, bf16[512,3072]{1,0:T(8,128)(2,1)} %get-tuple-element.11.upper_far, bf16[5,256,256]{2,1,0:T(8,128)(2,1)} %get-tuple-element.12.factors), custom_call_target="tpu_custom_call" | custom-call | tf_op jit(solution)/shard_map/reduce_layers/pallas_call | solution.py:457
  217.6 2.4 %copy.5 = f32[1,1,96,3072]{3,2,1,0:T(8,128)} copy(f32[1,1,96,3072]{3,2,1,0:T(8,128)} %bitcast.6) | data formatting | bytes 2359296

commit v2 on v1

v2 whole, which is shorter than its diff:
```python
import jax
import jax.numpy as jnp
from jax import lax
from jax.experimental import pallas as pl
from jax.experimental.pallas import tpu as pltpu
from jax.sharding import PartitionSpec as P

W = 256
NB = 24
ROWS = 3072
SHARE = 96
UNIT = 128
COUNTS = (5, 4, 1, 1)
BASES = tuple(sum(COUNTS[:k]) for k in range(4))
MAIN = COUNTS[0] + COUNTS[1]
SIDE = COUNTS[2] + COUNTS[3]
SLOTS = 2
SIDE_ORDER = ((3, 0), (2, 0))
LAGS = (2, 3, 4, 5)
SIDE_STEPS = (3, 4)
MIB = 2**20
MESH = pl.DeviceIdType.MESH
F32 = jnp.float32
BF16 = jnp.bfloat16


def dot(left, right):
    return jnp.dot(left, right, preferred_element_type=F32)


def split(value):
    high = value.astype(BF16)
    return high, (value - high.astype(F32)).astype(BF16)


def place():
    rep, row, col = (lax.axis_index(name) for name in ("rep", "row", "col"))
    return rep // 8, (rep // 2) % 4, rep % 2, row, col


def device(z, y, x, row, col):
    return {"rep": z * 8 + y * 2 + x, "row": row, "col": col}


def gather_kernel(front, corners, strip_far, send_sem, recv_sem, copy_sem):
    z, y, x, row, col = place()
    beside = device(z, y, x, 1 - row, col)
    across = device(z, y, x, row, 1 - col)
    barrier = pltpu.get_barrier_semaphore()
    for peer in (beside, across):
        pl.semaphore_signal(barrier, inc=1, device_id=peer, device_id_type=MESH)
    pl.semaphore_wait(barrier, 2)
    corner = front.at[pl.ds(row * W, W), pl.ds(col * W, W)]
    strip = front.at[pl.ds(row * W, W), :]

    def remote(src, dst, index, peer):
        return pltpu.make_async_remote_copy(
            src_ref=src, dst_ref=dst, send_sem=send_sem.at[index], recv_sem=recv_sem.at[index],
            device_id=peer, device_id_type=MESH)

    mine = row * 2 + col
    first = remote(corner, corners.at[mine], 0, across)
    first.start()
    second = remote(corner, corners.at[mine], 1, beside)
    second.start()
    third = remote(strip, strip_far, 2, beside)
    third.start()
    own_corner = pltpu.make_async_copy(corner, corners.at[mine], copy_sem.at[0])
    own_corner.start()
    first.wait_recv()
    theirs = row * 2 + 1 - col
    fourth = remote(corners.at[theirs], corners.at[theirs], 3, beside)
    fourth.start()
    first.wait_send()
    second.wait()
    third.wait()
    fourth.wait()
    own_corner.wait()


def invert(pivot, pivot_high, pivot_low, high, low, work):
    rows = lax.broadcasted_iota(jnp.int32, (W, W), 0)
    cols = lax.broadcasted_iota(jnp.int32, (W, W), 1)
    eye = rows == cols
    ones = jnp.where(eye, 1.0, 0.0)
    diag = jnp.where(eye, pivot, 0.0)
    down = jnp.sum(diag, axis=1, keepdims=True)
    along = jnp.sum(diag, axis=0, keepdims=True)
    rest = jnp.where(eye, 0.0, -pivot / along)
    rest_low = rest.astype(BF16)
    guess = (ones + rest) / down
    two = dot(rest_low, rest_low).astype(BF16)
    four = dot(two, two).astype(BF16)
    guess = guess + dot(guess.astype(BF16), two)
    guess = guess + dot(guess.astype(BF16), four)
    guess_high, guess_low = split(guess)
    product = dot(pivot_high, guess_high) + dot(pivot_high, guess_low)
    if pivot_low is not None:
        product = product + dot(pivot_low, guess_high)
    residual = ones - product
    guess = guess + dot(guess_high, residual.astype(BF16))
    size = jnp.max(jnp.sum(jnp.abs(residual), axis=1))
    good = size < 0.03
    work[...] = guess

    @pl.when(jnp.logical_not(good))
    def _():
        work[...] = pivot

        def step(k, carry):
            here = work[...]
            across = work[pl.ds(k, 1), :]
            column = jnp.sum(jnp.where(cols == k, here, 0.0), axis=1, keepdims=True)
            lane = lax.broadcasted_iota(jnp.int32, (1, W), 1) == k
            value = jnp.sum(jnp.where(lane, across, 0.0), axis=1, keepdims=True)
            scaled = jnp.where(lane, 1.0, across) / value
            here = jnp.where(cols == k, 0.0, here) - column * scaled
            work[...] = jnp.where(rows == k, scaled, here)
            return carry

        lax.fori_loop(0, W, step, 0)

    result_high, result_low = split(work[...])
    high[...] = result_high
    low[...] = result_low


def factor_kernel(lower_mask, upper_mask, front, corners, strip_far, factors, upper_far, work,
                  strips, upper, in_sem, out_sem):
    row, col = lax.axis_index("row"), lax.axis_index("col")

    def strip_copy(part):
        if part == 0:
            source, slot = front.at[pl.ds(pl.multiple_of(row * W, W), W), :], row
        else:
            source, slot = strip_far, 1 - row
        return pltpu.make_async_copy(source, strips.at[slot], in_sem.at[part])

    def upper_copy(block):
        span = pl.ds(block * W, W)
        return pltpu.make_async_copy(upper.at[:, span], upper_far.at[:, span], out_sem.at[block])

    for part in range(2):
        strip_copy(part).start()
    zero_high, zero_low, one_high, one_low = (factors.at[k] for k in range(4))
    invert(corners[0].astype(F32), corners[0], None, zero_high, zero_low, work)
    keep_low = lower_mask[0, 0, NB // 2 + 1].astype(F32)
    keep_up = upper_mask[0, 0, NB // 2 + 1].astype(F32)
    below = dot(corners[2], zero_high[...]) + dot(corners[2], zero_low[...])
    below = (below * keep_low).astype(BF16)
    right = (corners[1].astype(F32) * keep_up).astype(BF16)
    factors[4] = right
    for part in range(2):
        strip_copy(part).wait()
    for block in range(NB // 2):
        span = pl.ds(block * W, W)
        mask_zero = upper_mask[0, 0, col * (NB // 2) + block].astype(F32)
        mask_one = upper_mask[0, 1, col * (NB // 2) + block].astype(F32)
        top = (strips[0, :, span].astype(F32) * mask_zero).astype(BF16)
        upper[0:W, span] = top
        under = strips[1, :, span].astype(F32) - dot(below, top)
        upper[W:2 * W, span] = (under * mask_one).astype(BF16)
        upper_copy(block).start()
    pivot = corners[3].astype(F32) - dot(below, right)
    pivot_high, pivot_low = split(pivot)
    invert(pivot, pivot_high, pivot_low, one_high, one_low, work)
    for block in range(NB // 2):
        upper_copy(block).wait()


class Refs:
    def __init__(self, *refs):
        (self.tile, self.snd_first, self.snd_one, self.rcv_one, self.snd_two, self.rcv_two,
         self.snd_wide, self.rcv_wide, self.held, self.tile_sem, self.first_sem, self.one_snd,
         self.one_rcv, self.two_snd, self.two_rcv) = refs


def reduce_kernel(lower_mask, front, upper_far, factors, out, upper, lower, strip, held_two,
                  snd_last, rcv_last, tile_x, snd_x, rcv_x, upper_sem, panel_sem, strip_sem,
                  last_snd, last_rcv, tile_x_sem, x_snd, x_rcv, *rest):
    main, side = Refs(*rest[:15]), Refs(*rest[15:])
    z, y, x, row, col = place()

    def at_z(k):
        return device((z + k + 4) % 4, y, x, row, col)

    def at_y(k):
        return device(z, (y + k + 4) % 4, x, row, col)

    first_at = (at_z, at_y, at_z, at_y)
    second_at = (at_y, at_z, at_y, at_z)
    first_pos = (z, y, z, y)
    second_pos = (y, z, y, z)
    pair = device(z, y, 1 - x, row, col)
    across = device(z, y, x, row, 1 - col)
    upper_copy = pltpu.make_async_copy(upper_far, upper, upper_sem.at[0])
    upper_copy.start()

    def refs_of(stream):
        return main if stream < 2 else side

    def own(stream, i):
        return BASES[stream] + i - (0 if stream < 2 else MAIN)

    def slot(stream, i):
        return stream * SLOTS + i % SLOTS if stream < 2 else own(stream, i)

    def depth_of(stream):
        return 2 * SHARE if stream < 2 else SHARE

    def span_of(stream, i):
        block = BASES[stream] + i
        start = W * (block + 1) - W * col * (1 - jnp.minimum(block, 1))
        return pl.ds(pl.multiple_of(start, W), W)

    def dest_of(stream, kind):
        return (first_pos[stream] + (2, 1, 3, 0)[kind]) % 4

    def rows_of(ref, stream, kind):
        dest = dest_of(stream, kind)
        return (ref.at[dest], ref.at[:, dest], ref.at[dest, :, x], ref.at[:, dest, x])[stream]

    def tile_copy(stream, kind, i):
        source = rows_of(front, stream, kind)
        source = source.at[(slice(None),) * (3 if stream < 2 else 2) + (span_of(stream, i),)]
        if stream < 2:
            target, sem = main.tile.at[stream, kind - 1, i % 2], main.tile_sem.at[stream, kind - 1, i % 2]
        else:
            target, sem = side.tile.at[own(stream, i), kind], side.tile_sem.at[own(stream, i), kind]
        return pltpu.make_async_copy(source, target, sem)

    def strip_copy(k):
        at, by = opening(k)
        return pltpu.make_async_copy(front.at[(z + at) % 4, (y + by) % 4], strip.at[k % 2],
                                     strip_sem.at[k % 2])

    cross_slot = [SIDE_ORDER.index((stream, i)) % 2 for stream in (2, 3) for i in range(COUNTS[stream])]

    def cross_copy(stream, i):
        source = front.at[:, :, 1 - x, :, span_of(stream, i)]
        index = cross_slot[own(stream, i)]
        return pltpu.make_async_copy(source, tile_x.at[index], tile_x_sem.at[index])

    def opening(k):
        far = ((k + 1) // 2 + 2) % 4
        odd = k % 2
        return odd * 2 + (1 - odd) * far, odd * far + (1 - odd) * 2

    later = (
        (3, lambda k: (1, (1 + 2 * k + 3 * (k // 2)) % 4)),
        (2, lambda k: (3 * (1 - k), 1)),
        (2, lambda k: (3, 3 * (1 - k))),
        (1, lambda k: (0, 3)),
        (1, lambda k: (0, 0)),
    )

    for k in range(2):
        strip_copy(k).start()

    barrier = pltpu.get_barrier_semaphore()
    for peer in (at_z(1), at_z(-1), at_y(1), at_y(-1), pair, across):
        pl.semaphore_signal(barrier, inc=1, device_id=peer, device_id_type=MESH)
    pl.semaphore_wait(barrier, 6)

    def loop(count, function):
        def body(k, carry):
            function(k)
            return carry
        lax.fori_loop(0, count, body, 0)

    def piece_copies(dz, dy):
        at, by = (z + dz) % 4, (y + dy) % 4
        span = pl.ds(pl.multiple_of(col * W, W), W)
        source = front.at[at, by, :, :, span]
        target = lower.at[at, by, :, :, span]
        here = pltpu.make_async_copy(source, target, panel_sem.at[0, dz, dy])
        remote = pltpu.make_async_remote_copy(
            src_ref=source, dst_ref=target, send_sem=panel_sem.at[1, dz, dy],
            recv_sem=panel_sem.at[2, dz, dy], device_id=across, device_id_type=MESH)
        return here, remote

    def send_piece(dz, dy):
        for copy in piece_copies(dz, dy):
            copy.start()

    def make_piece(dz, dy):
        for copy in piece_copies(dz, dy):
            copy.wait()
        at, by = (z + dz) % 4, (y + dy) % 4
        cell = by * 192 + lax.broadcasted_iota(jnp.int32, (192, W), 0)

        def keep(section):
            first = row * (NB // 2) + at * 3
            flags = [lower_mask[0, section, first + part].astype(F32) for part in range(3)]
            return jnp.where(cell < W, flags[0], jnp.where(cell < 2 * W, flags[1], flags[2]))

        left = lower[at, by, :, :, 0:W].reshape(192, W)
        column = lower[at, by, :, :, W:2 * W].reshape(192, W).astype(F32)
        first = dot(left, factors[0]) + dot(left, factors[1])
        first = (first * keep(0)).astype(BF16)
        column_high, column_low = split(column - dot(first, factors[4]))
        second = (dot(column_high, factors[2]) + dot(column_high, factors[3])
                  + dot(column_low, factors[2]))
        second = (second * keep(1)).astype(BF16)
        lower[at, by, :, :, 0:W] = first.reshape(2, SHARE, W)
        lower[at, by, :, :, W:2 * W] = second.reshape(2, SHARE, W)

    loop(7, lambda k: send_piece(*opening(k)))
    for count, spot in later:
        loop(count, lambda k, spot=spot: send_piece(*spot(k)))
    for kind in (1, 2, 3):
        for stream in range(2):
            tile_copy(stream, kind, 0).start()
    for stream, i in SIDE_ORDER[:2]:
        cross_copy(stream, i).start()
    for stream in (2, 3):
        for i in range(COUNTS[stream]):
            for kind in range(4):
                tile_copy(stream, kind, i).start()

    def product(stream, kind, i):
        rows = 4 * depth_of(stream)
        if stream < 2:
            @pl.when(i + 1 < COUNTS[stream])
            def _():
                tile_copy(stream, kind, i + 1).start()
            held = main.tile.at[stream, kind - 1, i % 2]
        else:
            held = side.tile.at[own(stream, i), kind]
        left = rows_of(lower, stream, kind)[...].reshape(rows, 2 * W)
        update = dot(left, upper[:, span_of(stream, i)])
        tile_copy(stream, kind, i).wait()
        value = held[...].reshape(rows, W).astype(F32) - update
        if stream >= 2:
            dest, block = dest_of(stream, kind), own(stream, i)
            other = rcv_x[block, dest] if stream == 2 else rcv_x[block, :, dest]
            value = value + other.reshape(rows, W).astype(F32)
        return value

    def half_of(value, half):
        return value[:, half * UNIT:half * UNIT + UNIT]

    def peer_of(places_of, half, kind):
        turn = 1 - 2 * half
        return places_of(turn if kind < 2 else -turn)

    def copy_one(stream, kind, half, i, part=None):
        refs, block = refs_of(stream), own(stream, i)
        if kind == 0:
            src, sem = refs.snd_first.at[block, half], refs.first_sem.at[block, half]
        else:
            src = refs.snd_one.at[block, kind - 1, half]
            sem = refs.one_snd.at[block, kind - 1, half]
        dst = refs.rcv_one.at[block, kind, half]
        if part is not None:
            src, dst = src.at[part], dst.at[part]
        return pltpu.make_async_remote_copy(
            src_ref=src, dst_ref=dst, send_sem=sem, recv_sem=refs.one_rcv.at[block, kind, half],
            device_id=peer_of(first_at[stream], half, kind), device_id_type=MESH)

    def send_one(stream, kind, half, i, value):
        refs, block = refs_of(stream), own(stream, i)
        value = value.astype(BF16).reshape(4, depth_of(stream), UNIT)
        if kind == 0:
            refs.snd_first[block, half] = value
        else:
            refs.snd_one[block, kind - 1, half] = value
        copy_one(stream, kind, half, i).start()

    def got_one(stream, kind, half, i):
        copy_one(stream, kind, half, i).wait_recv()
        value = refs_of(stream).rcv_one[own(stream, i), kind, half]
        return value.reshape(4 * depth_of(stream), UNIT).astype(F32)

    def copy_two(stream, kind, half, i):
        refs, block, index = refs_of(stream), own(stream, i), slot(stream, i)
        if kind == 0:
            src, dst = refs.snd_two.at[index, half], refs.rcv_two.at[block, half]
        else:
            src = refs.snd_wide.at[index, kind - 1, half]
            dst = refs.rcv_wide.at[block, kind - 1, half]
        return pltpu.make_async_remote_copy(
            src_ref=src, dst_ref=dst, send_sem=refs.two_snd.at[index, kind, half],
            recv_sem=refs.two_rcv.at[block, kind, half],
            device_id=peer_of(second_at[stream], half, kind), device_id_type=MESH)

    def send_two(stream, kind, half, i, value):
        refs, index = refs_of(stream), slot(stream, i)
        if stream < 2:
            @pl.when(i >= SLOTS)
            def _():
                copy_two(stream, kind, half, i - SLOTS).wait_send()
        if kind == 0:
            refs.snd_two[index, half] = value.astype(BF16)
        else:
            refs.snd_wide[index, kind - 1, half] = value
        copy_two(stream, kind, half, i).start()

    def copy_last(stream, i):
        index, block = slot(stream, i), own(stream, i)
        return pltpu.make_async_remote_copy(
            src_ref=snd_last.at[index], dst_ref=rcv_last.at[block], send_sem=last_snd.at[index],
            recv_sem=last_rcv.at[block], device_id=pair, device_id_type=MESH)

    def copy_cross(stream, i):
        block = own(stream, i)
        return pltpu.make_async_remote_copy(
            src_ref=snd_x.at[block], dst_ref=rcv_x.at[block], send_sem=x_snd.at[block],
            recv_sem=x_rcv.at[block], device_id=pair, device_id_type=MESH)

    def open_piece(stream, at, by, k):
        part = by if stream == 0 else at

        def body(i, carry):
            span = span_of(stream, i)
            value = strip[k % 2, :, :, span].reshape(192, W).astype(F32)
            value = value - dot(lower[at, by].reshape(192, 2 * W), upper[:, span])
            for half in range(2):
                main.snd_first[own(stream, i), half, part] = half_of(value, half).astype(BF16)
                copy_one(stream, 0, half, i, part).start()
            return carry
        lax.fori_loop(0, COUNTS[stream], body, 0)

    def open_pieces(k):
        dz, dy = opening(k)
        at, by = (z + dz) % 4, (y + dy) % 4
        make_piece(dz, dy)
        strip_copy(k).wait()

        @pl.when((k == 0) | (k % 2 == 1))
        def _():
            open_piece(0, at, by, k)

        @pl.when(k % 2 == 0)
        def _():
            open_piece(1, at, by, k)

        @pl.when(k + 2 < 7)
        def _():
            strip_copy(k + 2).start()

    def cross_block(stream, i):
        cross_copy(stream, i).wait()
        block = own(stream, i)
        for part in range(2):
            span = pl.ds(2 * part, 2)
            left = lower[span, :, 1 - x].reshape(768, 2 * W)
            value = tile_x[cross_slot[block], span].reshape(768, W).astype(F32)
            value = value - dot(left, upper[:, span_of(stream, i)])
            snd_x[block, span] = value.astype(BF16).reshape(2, 4, SHARE, W)
        copy_cross(stream, i).start()

    def open_block(stream, i):
        copy_cross(stream, i).wait_recv()
        value = product(stream, 0, i)
        for half in range(2):
            send_one(stream, 0, half, i, half_of(value, half))

    def pass_side(stream, ahead, i):
        value = product(stream, 1 + ahead, i)
        send_one(stream, 2, 1 - ahead, i, half_of(value, 1 - ahead))
        send_one(stream, 1, ahead, i, half_of(value, ahead) + got_one(stream, 0, ahead, i))

    def pass_block(stream, i):
        pass_side(stream, 0, i)
        pass_side(stream, 1, i)

    def close_block(stream, i):
        refs, index, depth = refs_of(stream), slot(stream, i), depth_of(stream)
        value = product(stream, 3, i)
        pos = second_pos[stream]
        for half in range(2):
            part = half_of(value, half) + got_one(stream, 2, half, i) + got_one(stream, 1, half, i)
            refs.held[index, half] = part.reshape(4, depth, UNIT)
            send_two(stream, 0, half, i, refs.held[index, half, (pos + 2) % 4])
            send_two(stream, 2, half, i, refs.held[index, half, (pos + 3 + 2 * half) % 4])

    def pass_sum(stream, i):
        refs, index, block = refs_of(stream), slot(stream, i), own(stream, i)
        for half in range(2):
            copy_two(stream, 0, half, i).wait_recv()
            value = refs.held[index, half, (second_pos[stream] + 1 + 2 * half) % 4]
            send_two(stream, 1, half, i, value + refs.rcv_two[block, half].astype(F32))

    def live(width):
        cells = (z * 8 + y * 2 + x) * SHARE + lax.broadcasted_iota(jnp.int32, (SHARE, width), 0)
        return (cells < row * W) | (cells >= row * W + W)

    def close_sum(stream, i):
        refs, index, block = refs_of(stream), slot(stream, i), own(stream, i)
        values = []
        for half in range(2):
            copy_two(stream, 2, half, i).wait_recv()
            copy_two(stream, 1, half, i).wait_recv()
            value = refs.held[index, half, second_pos[stream]]
            values.append(value + refs.rcv_wide[block, 0, half] + refs.rcv_wide[block, 1, half])
        value = jnp.concatenate(values, axis=1)
        if stream >= 2:
            out[:, span_of(stream, i)] = jnp.where(live(W), value, 0.0)
            return
        held_two[index] = value.reshape(2, SHARE, W)

        @pl.when(i >= SLOTS)
        def _():
            copy_last(stream, i - SLOTS).wait_send()
        snd_last[index] = held_two[index, 1 - x]
        copy_last(stream, i).start()

    def finish(stream, i):
        copy_last(stream, i).wait_recv()
        value = held_two[slot(stream, i), x] + rcv_last[own(stream, i)]
        out[:, span_of(stream, i)] = jnp.where(live(W), value, 0.0)

    upper_copy.wait()
    loop(7, open_pieces)
    turns = ((0, 0), (1, 0), (0, 1), (1, 1))
    for k, (count, spot) in enumerate(later):
        loop(count, lambda k, spot=spot: make_piece(*spot(k)))
        if k < len(turns):
            pass_side(*turns[k], 0)
    out[:, pl.ds(pl.multiple_of(col * W, W), W)] = jnp.zeros((SHARE, W), F32)

    def when(function, stream, i):
        @pl.when((i >= 0) & (i < COUNTS[stream]))
        def _():
            function(stream, i)

    def step(now):
        for stream in range(2):
            when(finish, stream, now - LAGS[3])
        for stream in range(2):
            when(close_sum, stream, now - LAGS[2])

        @pl.when(now > 0)
        def _():
            for ahead in range(2):
                for stream in range(2):
                    when(lambda stream, i, ahead=ahead: pass_side(stream, ahead, i), stream, now)
        for k, (stream, i) in enumerate(SIDE_ORDER):
            @pl.when(now == k)
            def _(stream=stream, i=i, k=k):
                cross_block(stream, i)
                if k + 2 < SIDE:
                    cross_copy(*SIDE_ORDER[k + 2]).start()
        for stream in range(2):
            when(pass_sum, stream, now - LAGS[1])
        for stream in range(2):
            when(close_block, stream, now - LAGS[0])
        for k, (stream, i) in enumerate(SIDE_ORDER):
            for shift, stage in enumerate((open_block, pass_block, close_block, pass_sum, close_sum)):
                @pl.when(now == SIDE_STEPS[k] + shift)
                def _(stage=stage, stream=stream, i=i):
                    stage(stream, i)

    loop(max(max(SIDE_STEPS) + 5, max(COUNTS) + LAGS[3]), step)

    for stream in range(4):
        for i in range(COUNTS[stream]):
            for half in range(2):
                for kind in range(3):
                    copy_one(stream, kind, half, i).wait_send()
                    if stream >= 2 or i >= COUNTS[stream] - SLOTS:
                        copy_two(stream, kind, half, i).wait_send()
            if stream >= 2:
                copy_cross(stream, i).wait_send()
            elif i >= COUNTS[stream] - SLOTS:
                copy_last(stream, i).wait_send()


def local(fronts, lower_mask, upper_mask):
    any_space = pl.BlockSpec(memory_space=pl.ANY)
    vmem = pl.BlockSpec(memory_space=pltpu.VMEM)
    smem = pl.BlockSpec(memory_space=pltpu.SMEM)
    front = fronts.reshape(ROWS, ROWS)
    dma = pltpu.SemaphoreType.DMA
    corners, strip = pl.pallas_call(
        gather_kernel,
        out_shape=[jax.ShapeDtypeStruct((4, W, W), BF16), jax.ShapeDtypeStruct((W, ROWS), BF16)],
        in_specs=[any_space],
        out_specs=[vmem, vmem],
        scratch_shapes=[dma((4,)), dma((4,)), dma((1,))],
        compiler_params=pltpu.CompilerParams(collective_id=0, has_side_effects=True,
                                             vmem_limit_bytes=60 * MIB),
        name="gather_corners",
    )(front)
    factors, upper = pl.pallas_call(
        factor_kernel,
        out_shape=[jax.ShapeDtypeStruct((5, W, W), BF16),
                   jax.ShapeDtypeStruct((2 * W, ROWS), BF16)],
        in_specs=[smem, smem, any_space, vmem, any_space],
        out_specs=[vmem, any_space],
        scratch_shapes=[pltpu.VMEM((W, W), F32), pltpu.VMEM((2, W, ROWS), BF16),
                        pltpu.VMEM((2 * W, ROWS), BF16), dma((2,)), dma((NB // 2,))],
        compiler_params=pltpu.CompilerParams(vmem_limit_bytes=60 * MIB),
        name="invert_pivots",
    )(lower_mask, upper_mask, front, corners, strip)
    def group(blocks, slots, depth, tile, rows):
        return [
            pltpu.VMEM(tile + rows + (W,), BF16),
            pltpu.VMEM((blocks, 2, 4, depth, UNIT), BF16),
            pltpu.VMEM((blocks, 2, 2, 4, depth, UNIT), BF16),
            pltpu.VMEM((blocks, 3, 2, 4, depth, UNIT), BF16),
            pltpu.VMEM((slots, 2, depth, UNIT), BF16),
            pltpu.VMEM((blocks, 2, depth, UNIT), BF16),
            pltpu.VMEM((slots, 2, 2, depth, UNIT), F32),
            pltpu.VMEM((blocks, 2, 2, depth, UNIT), F32),
            pltpu.VMEM((slots, 2, 4, depth, UNIT), F32),
            dma(tile), dma((blocks, 2)), dma((blocks, 2, 2)), dma((blocks, 3, 2)),
            dma((slots, 3, 2)), dma((blocks, 3, 2)),
        ]

    main = group(MAIN, 2 * SLOTS, 2 * SHARE, (2, 3, 2), (4, 2, SHARE))
    side = group(SIDE, SIDE, SHARE, (SIDE, 4), (4, SHARE))
    out = pl.pallas_call(
        reduce_kernel,
        out_shape=jax.ShapeDtypeStruct((SHARE, ROWS), F32),
        in_specs=[smem, any_space, any_space, vmem],
        out_specs=vmem,
        scratch_shapes=[
            pltpu.VMEM((2 * W, ROWS), BF16),
            pltpu.VMEM((4, 4, 2, SHARE, 2 * W), BF16),
            pltpu.VMEM((2, 2, SHARE, ROWS), BF16),
            pltpu.VMEM((2 * SLOTS, 2, SHARE, W), F32),
            pltpu.VMEM((2 * SLOTS, SHARE, W), F32),
            pltpu.VMEM((MAIN, SHARE, W), F32),
            pltpu.VMEM((2, 4, 4, SHARE, W), BF16),
            pltpu.VMEM((SIDE, 4, 4, SHARE, W), BF16),
            pltpu.VMEM((SIDE, 4, 4, SHARE, W), BF16),
            dma((1,)), dma((3, 4, 4)), dma((2,)), dma((2 * SLOTS,)), dma((MAIN,)), dma((2,)),
            dma((SIDE,)), dma((SIDE,)),
        ] + main + side,
        compiler_params=pltpu.CompilerParams(collective_id=1, has_side_effects=True,
                                             vmem_limit_bytes=63 * MIB),
        name="reduce_layers",
    )(lower_mask, front.reshape(4, 4, 2, SHARE, ROWS), upper, factors)
    return out.reshape(1, 1, SHARE, ROWS)


def solution(mesh):
    in_specs = (P("rep", "row", "col"), P("rep", None, None), P("rep", None, None))
    out_specs = P("row", "rep", None, "col")
    return jax.shard_map(local, mesh=mesh, in_specs=in_specs, out_specs=out_specs, check_vma=False)
```

time: 221 us -> 211 us (0.955)
  Pallas kernels: 218 us -> 208 us
    pallas_call x1, Pallas kernels: 136 us -> 127 us  [local(): pl.pallas_call(reduce_kernel, out_shape=jax.ShapeDtypeStruct((SHARE, ROWS...]
where the time goes in v2:
time: 211 us
  Pallas kernels  208 us (99%)
  local copies, waits for them, and re-layouts  2.36 us (1%)
    pallas_call x1, Pallas kernels, local(): pl.pallas_call(reduce_kernel, out_shape=jax.ShapeDtypeStruct((SHARE, ROWS...  127 us
    pallas_call x1, Pallas kernels, local(): pl.pallas_call(factor_kernel, out_shape=[jax.ShapeDtypeStruct((5, W, W),...  71.8 us
    pallas_call x1, Pallas kernels, local(): pl.pallas_call(gather_kernel, out_shape=[jax.ShapeDtypeStruct((4, W, W),...  9.89 us

profile of v2, /device:TPU:0, one launch (start us, length us, event | category | flops | bytes accessed | tf_op | source)
XLA Modules:
  0.0 210.9 jit_solution(4926879809914643545)
XLA Ops:
  0.0 9.9 %gather_corners.1 = (bf16[4,256,256]{2,1,0:T(8,128)(2,1)}, bf16[256,3072]{1,0:T(8,128)(2,1)}) custom-call(bf16[3072,3072]{1,0:T(8,128)(2,1)} %bitcast.3), custom_call_target="tpu_custom_call" | custom-call | tf_op jit(solution)/shard_map/gather_corners/pallas_call | solution.py:576
  9.9 71.8 %invert_pivots.1 = (bf16[5,256,256]{2,1,0:T(8,128)(2,1)}, bf16[512,3072]{1,0:T(8,128)(2,1)}) custom-call(s32[1,2,24]{2,1,0:T(2,128)} %lower_mask.3, s32[1,2,24]{2,1,0:T(2,128)} %upper_mask.1, bf16[3072,3072]{1,0:T(8,128)(2,1)} %bitcast.4, bf16[4,256,256]{2,1,0:T(8,128)(2,1)} %get-tuple-element.9.corners, bf16[256,3072]{1,0:T(8,128)(2,1)} %get-tuple-element.10.strip_far), custom_call_target="tpu_custom_call" | custom-call | tf_op jit(solution)/shard_map/invert_pivots/pallas_call | solution.py:586
  81.7 126.8 %reduce_layers.1 = f32[96,3072]{1,0:T(8,128)} custom-call(s32[1,2,24]{2,1,0:T(2,128)} %lower_mask.3, bf16[4,4,2,96,3072]{4,3,2,1,0:T(8,128)(2,1)} %bitcast.5, bf16[512,3072]{1,0:T(8,128)(2,1)} %get-tuple-element.11.upper_far, bf16[5,256,256]{2,1,0:T(8,128)(2,1)} %get-tuple-element.12.factors), custom_call_target="tpu_custom_call" | custom-call | tf_op jit(solution)/shard_map/reduce_layers/pallas_call | solution.py:614
  208.5 2.4 %copy.5 = f32[1,1,96,3072]{3,2,1,0:T(8,128)} copy(f32[1,1,96,3072]{3,2,1,0:T(8,128)} %bitcast.6) | data formatting | bytes 2359296

commit v3 on v2

--- a/solution.py
+++ b/solution.py
@@ -526,10 +526,6 @@
             function(stream, i)
 
     def step(now):
-        for stream in range(2):
-            when(finish, stream, now - LAGS[3])
-        for stream in range(2):
-            when(close_sum, stream, now - LAGS[2])
 
         @pl.when(now > 0)
         def _():
@@ -542,6 +538,10 @@
                 cross_block(stream, i)
                 if k + 2 < SIDE:
                     cross_copy(*SIDE_ORDER[k + 2]).start()
+        for stream in range(2):
+            when(finish, stream, now - LAGS[3])
+        for stream in range(2):
+            when(close_sum, stream, now - LAGS[2])
         for stream in range(2):
             when(pass_sum, stream, now - LAGS[1])
         for stream in range(2):

time: 211 us -> 210 us (level)
  no operation moved by 1% of the time
where the time goes in v3:
time: 210 us; the launch traced here: 209 us
  Pallas kernels  207 us (99%)
  local copies, waits for them, and re-layouts  2.36 us (1%)
    pallas_call x1, Pallas kernels, local(): pl.pallas_call(reduce_kernel, out_shape=jax.ShapeDtypeStruct((SHARE, ROWS...  125 us
    pallas_call x1, Pallas kernels, local(): pl.pallas_call(factor_kernel, out_shape=[jax.ShapeDtypeStruct((5, W, W),...  71.8 us
    pallas_call x1, Pallas kernels, local(): pl.pallas_call(gather_kernel, out_shape=[jax.ShapeDtypeStruct((4, W, W),...  9.89 us

profile of v3, /device:TPU:0, one launch (start us, length us, event | category | flops | bytes accessed | tf_op | source)
XLA Modules:
  0.0 209.4 jit_solution(16681649847290747674)
XLA Ops:
  0.0 9.9 %gather_corners.1 = (bf16[4,256,256]{2,1,0:T(8,128)(2,1)}, bf16[256,3072]{1,0:T(8,128)(2,1)}) custom-call(bf16[3072,3072]{1,0:T(8,128)(2,1)} %bitcast.3), custom_call_target="tpu_custom_call" | custom-call | tf_op jit(solution)/shard_map/gather_corners/pallas_call | solution.py:576
  9.9 71.8 %invert_pivots.1 = (bf16[5,256,256]{2,1,0:T(8,128)(2,1)}, bf16[512,3072]{1,0:T(8,128)(2,1)}) custom-call(s32[1,2,24]{2,1,0:T(2,128)} %lower_mask.3, s32[1,2,24]{2,1,0:T(2,128)} %upper_mask.1, bf16[3072,3072]{1,0:T(8,128)(2,1)} %bitcast.4, bf16[4,256,256]{2,1,0:T(8,128)(2,1)} %get-tuple-element.9.corners, bf16[256,3072]{1,0:T(8,128)(2,1)} %get-tuple-element.10.strip_far), custom_call_target="tpu_custom_call" | custom-call | tf_op jit(solution)/shard_map/invert_pivots/pallas_call | solution.py:586
  81.7 125.3 %reduce_layers.1 = f32[96,3072]{1,0:T(8,128)} custom-call(s32[1,2,24]{2,1,0:T(2,128)} %lower_mask.3, bf16[4,4,2,96,3072]{4,3,2,1,0:T(8,128)(2,1)} %bitcast.5, bf16[512,3072]{1,0:T(8,128)(2,1)} %get-tuple-element.11.upper_far, bf16[5,256,256]{2,1,0:T(8,128)(2,1)} %get-tuple-element.12.factors), custom_call_target="tpu_custom_call" | custom-call | tf_op jit(solution)/shard_map/reduce_layers/pallas_call | solution.py:614
  207.1 2.4 %copy.5 = f32[1,1,96,3072]{3,2,1,0:T(8,128)} copy(f32[1,1,96,3072]{3,2,1,0:T(8,128)} %bitcast.6) | data formatting | bytes 2359296
